TPU v7x, 256 devices: a whole 4x4x8 slice. The times are simulated.
256 devices in a mesh: row: 64 (over z, y_hi, x), ka: 4 (over y_lo, core).
Axes of the slice: x: 4, y: 4 (y_hi: 2, y_lo: 2; y = y_hi * 2 + y_lo), z: 8, core: 2. Of those that a mesh axis runs over, the one named last changes fastest.
Arguments:
- pair: bfloat16 [256, 256, 128], P('row', 'ka'), may hold values from -6 to 6
- token_mask: int32 [256], replicated, may hold values 0 or 1
- w_proj: bfloat16 [2, 128, 640], replicated, may hold values from -0.5 to 0.5
- w_out: bfloat16 [2, 128, 128], replicated, may hold values from -0.5 to 0.5
Outputs:
- pair_out: bfloat16 [256, 256, 128], P('row', 'ka')
Inputs may be any that keep to these rules, and one draw needn't show every extreme that they name: `token_mask`: 1 marks a real token, 0 a padding token.
All inputs are finite; a program needn't handle non-finite values.
Results may differ from a plain program's by a relative error of at most 0.018.
Values may be sent and summed in bfloat16 or wider, within the bound.
A program may use at most 64 MiB of HBM per device.

v0:
```python
import jax
import jax.numpy as jnp
from jax import lax
from jax.sharding import PartitionSpec as P

epsilon = 1e-05


def normalize(values):
    mean = jnp.mean(values, axis=-1, keepdims=True)
    centered = values - mean
    variance = jnp.mean(centered * centered, axis=-1, keepdims=True)
    return centered * lax.rsqrt(variance + epsilon)


def project_block(normed, weights):
    lead = normed.shape[:2]
    flat = jnp.dot(normed.reshape(-1, normed.shape[2]), weights, preferred_element_type=jnp.float32)
    return flat.reshape(lead[0], lead[1], weights.shape[1])


def gated_sides(projected, pair_mask, hidden):
    left_side = (
        jax.nn.sigmoid(projected[..., :hidden])
        * projected[..., hidden : 2 * hidden]
        * pair_mask[..., None]
    )
    right_side = (
        jax.nn.sigmoid(projected[..., 2 * hidden : 3 * hidden])
        * projected[..., 3 * hidden : 4 * hidden]
        * pair_mask[..., None]
    )
    return (left_side.astype(jnp.bfloat16), right_side.astype(jnp.bfloat16))


def finish(pair, gate_out, summed, weights):
    xnorm = normalize(summed).astype(jnp.bfloat16)
    update = project_block(xnorm, weights)
    return (pair.astype(jnp.float32) + gate_out * update).astype(jnp.bfloat16)


def body(pair, token_mask, w_proj, w_out):
    row_count, col_count, pair_width = pair.shape
    hidden = w_out.shape[1]
    row_start = lax.axis_index("row") * row_count
    col_start = lax.axis_index("ka") * col_count
    token_weights = token_mask.astype(jnp.float32)
    mask_rows = lax.dynamic_slice_in_dim(token_weights, row_start, row_count)
    mask_cols = lax.dynamic_slice_in_dim(token_weights, col_start, col_count)
    pair_mask = mask_rows[:, None] * mask_cols[None, :]
    normed = normalize(pair.astype(jnp.float32)).astype(jnp.bfloat16)
    projected = project_block(normed, w_proj[0])
    left_side, right_side = gated_sides(projected, pair_mask, hidden)
    gate_out = jax.nn.sigmoid(projected[..., 4 * hidden :])
    terms = jnp.einsum(
        "ikc,jkc->ijc",
        left_side,
        lax.all_gather(right_side, "row", axis=0, tiled=True),
        preferred_element_type=jnp.float32,
    )
    summed = lax.psum_scatter(
        terms.astype(jnp.bfloat16), "ka", scatter_dimension=1, tiled=True
    ).astype(jnp.float32)
    pair = finish(pair, gate_out, summed, w_out[0])
    normed = normalize(pair.astype(jnp.float32)).astype(jnp.bfloat16)
    projected = project_block(normed, w_proj[1])
    left_side, right_side = gated_sides(projected, pair_mask, hidden)
    gate_out = jax.nn.sigmoid(projected[..., 4 * hidden :])
    spread_left, spread_right = (
        lax.all_to_all(left_side, "ka", split_axis=0, concat_axis=1, tiled=True),
        lax.all_to_all(right_side, "ka", split_axis=0, concat_axis=1, tiled=True),
    )
    left_moved, right_moved = (
        lax.all_to_all(spread_left, "row", split_axis=1, concat_axis=0, tiled=True),
        lax.all_to_all(spread_right, "row", split_axis=1, concat_axis=0, tiled=True),
    )
    terms = jnp.einsum(
        "kic,kjc->ijc",
        left_moved,
        lax.all_gather(right_moved, "row", axis=1, tiled=True),
        preferred_element_type=jnp.float32,
    )
    summed = lax.psum_scatter(
        terms.astype(jnp.bfloat16), "ka", scatter_dimension=1, tiled=True
    ).astype(jnp.float32)
    return finish(pair, gate_out, summed, w_out[1])


def solution(mesh):
    return jax.shard_map(
        body,
        mesh=mesh,
        in_specs=(P("row", "ka", None), P(), P(), P()),
        out_specs=P("row", "ka", None),
        check_vma=False,
    )
```

profile of v0, /device:TPU:1, one launch (start us, length us, event | category | flops | bytes accessed | tf_op | source)
XLA Modules:
  0.0 426.9 jit_solution(6153360204093187775)
XLA Ops:
  6.5 0.7 convert_element_type.61
  7.4 0.9 convert_reduce_fusion
  8.3 1.0 fusion.23
  9.4 1.3 fusion.9
  10.7 0.7 fusion.39
  11.7 128.1 %all-gather.3.cloned.1.call-done = bf16[256,64,128]{2,1,0:T(8,128)(2,1)} async-done(((bf16[4,64,128]{2,1,0:T(8,128)(2,1)}), bf16[256,64,128]{2,1,0:T(8,128)(2,1)}) %all-gather.3.cloned.1.call-update) | async-done | bytes 4194320 | tf_op jit(solution)/shard_map/all_gather | solution.py:58
  139.8 12.9 %copy.45 = bf16[256,64,128]{1,0,2:T(8,128)(2,1)} copy(bf16[256,64,128]{2,1,0:T(8,128)(2,1)} %all-gather.3.cloned.1.call-done) | data formatting | bytes 8388608 | tf_op jit(solution)/shard_map/all_gather | solution.py:58
  152.7 5.7 %fusion = bf16[4,256,128]{1,0,2:T(4,128)(2,1)S(1)} fusion(bf16[256,64,128]{1,0,2:T(8,128)(2,1)} %copy.45, bf16[4,64,128]{1,0,2:T(4,128)(2,1)S(1)} %copy.46), kind=kOutput, calls=%fused_computation.2 | convolution fusion | flops 16908288 | bytes 4521984 | tf_op jit(solution)/shard_map/ikc,jkc->ijc/dot_general | solution.py:55
  158.4 0.9 copy.47
  159.4 0.6 dynamic-slice
  160.7 40.6 %all-reduce.5.cloned.1.call-done = bf16[4,256,128]{2,0,1:T(4,128)(2,1)} async-done(((bf16[4,256,128]{2,0,1:T(4,128)(2,1)}), bf16[4,256,128]{2,0,1:T(4,128)(2,1)}) %all-reduce.5.cloned.1.call-update) | async-done | bytes 262160
  201.3 1.0 convert_reduce_fusion.2
  202.3 1.1 fusion.21
  203.4 1.0 fusion.22
  204.9 0.3 fusion.7
  205.3 5.8 %all_to_all.48 = bf16[4,64,128]{2,1,0:T(8,128)(2,1)S(1)} all-to-all(bf16[4,64,128]{2,1,0:T(8,128)(2,1)S(1)} %get-tuple-element.6), channel_id=1, replica_groups=mesh['row'=64,'ka'=4] {'ka'}, dimensions={0} | all-to-all | bytes 131072 | tf_op jit(solution)/shard_map/all_to_all | solution.py:71
  211.2 0.6 broadcast.123
  211.8 1.1 reduce
  212.9 23.1 %all_to_all.49 = bf16[64,2,256]{2,1,0:T(2,128)(2,1)S(1)} all-to-all(bf16[64,2,256]{2,1,0:T(2,128)(2,1)S(1)} %reshape.109), channel_id=1, replica_groups=mesh['row'=64,'ka'=4] {'row'}, dimensions={0} | all-to-all | bytes 131072 | tf_op jit(solution)/shard_map/all_to_all | solution.py:75
  236.1 0.6 copy.54
  236.8 7.9 %all_to_all.50 = bf16[4,64,128]{2,1,0:T(8,128)(2,1)S(1)} all-to-all(bf16[4,64,128]{2,1,0:T(8,128)(2,1)S(1)} %get-tuple-element.5), channel_id=1, replica_groups=mesh['row'=64,'ka'=4] {'ka'}, dimensions={0} | all-to-all | bytes 131072 | tf_op jit(solution)/shard_map/all_to_all | solution.py:70
  244.8 1.1 reduce.1
  245.9 14.8 %all_to_all.51 = bf16[64,2,256]{2,1,0:T(2,128)(2,1)S(1)} all-to-all(bf16[64,2,256]{2,1,0:T(2,128)(2,1)S(1)} %reshape.111), channel_id=1, replica_groups=mesh['row'=64,'ka'=4] {'row'}, dimensions={0} | all-to-all | bytes 131072 | tf_op jit(solution)/shard_map/all_to_all | solution.py:74
  260.9 94.3 %all-gather.5.cloned.1.call-done = bf16[64,256,128]{2,0,1:T(8,128)(2,1)} async-done(((bf16[64,4,128]{2,0,1:T(8,128)(2,1)}), bf16[64,256,128]{2,0,1:T(8,128)(2,1)}) %all-gather.5.cloned.1.call-update) | async-done | bytes 4194320 | tf_op jit(solution)/shard_map/all_gather | solution.py:80
  355.2 12.9 %copy.56 = bf16[64,256,128]{0,1,2:T(8,128)(2,1)} copy(bf16[64,256,128]{2,0,1:T(8,128)(2,1)} %all-gather.5.cloned.1.call-done) | data formatting | bytes 8388608 | tf_op jit(solution)/shard_map/all_gather | solution.py:80
  368.1 5.6 %fusion.1 = bf16[4,256,128]{1,0,2:T(4,128)(2,1)S(1)} fusion(bf16[64,256,128]{0,1,2:T(8,128)(2,1)} %copy.56, bf16[64,4,128]{0,1,2:T(4,128)(2,1)S(1)} %copy.57), kind=kOutput, calls=%fused_computation.3 | convolution fusion | flops 16908288 | bytes 4521984 | tf_op jit(solution)/shard_map/kic,kjc->ijc/dot_general | solution.py:77
  373.7 0.9 copy.58
  374.7 41.7 %all-reduce.7.cloned.1.call-done = bf16[4,256,128]{2,0,1:T(4,128)(2,1)} async-done(((bf16[4,256,128]{2,0,1:T(4,128)(2,1)}), bf16[4,256,128]{2,0,1:T(4,128)(2,1)}) %all-reduce.7.cloned.1.call-update) | async-done | bytes 262160
  416.4 1.0 convert_reduce_fusion.1
  417.4 1.1 fusion.19
  418.5 1.0 fusion.20
  419.6 0.8 fusion.5
  (40 shorter events, 1.8 us)
Async XLA Ops:
  6.5 133.3 %all-gather.3.cloned.1.call-start = ((), (), s32[]{:S(2)}) async-start(), calls=%async_computation.4 | async-start | bytes 4259840 | tf_op jit(solution)/shard_map/all_gather | solution.py:58
  11.5 189.8 %all-reduce.5.cloned.1.call-start = ((), (), s32[]{:S(2)}) async-start(), calls=%async_computation.6 | async-start | bytes 524288
  11.7 147.7 %copy-start.3 = (u32[256]{0:T(256)S(1)}, u32[256]{0:T(256)}, u32[]{:S(2)}) copy-start(u32[256]{0:T(256)} %constant.36) | copy-start | bytes 3076
  11.7 192.7 %copy-start = (bf16[4,64,128]{2,1,0:T(8,128)(2,1)S(1)}, bf16[4,64,128]{2,1,0:T(8,128)(2,1)}, u32[]{:S(2)}) copy-start(bf16[4,64,128]{2,1,0:T(8,128)(2,1)} %param.4) | copy-start | bytes 196612
  11.7 192.7 %copy-start.2 = (bf16[2,128,128]{2,1,0:T(8,128)(2,1)S(1)}, bf16[2,128,128]{2,1,0:T(8,128)(2,1)}, u32[]{:S(2)}) copy-start(bf16[2,128,128]{2,1,0:T(8,128)(2,1)} %param.7) | copy-start | bytes 196612
  152.7 52.2 %copy-start.1 = (bf16[2,128,640]{2,1,0:T(8,128)(2,1)S(1)}, bf16[2,128,640]{2,1,0:T(8,128)(2,1)}, u32[]{:S(2)}) copy-start(bf16[2,128,640]{2,1,0:T(8,128)(2,1)} %param.6) | copy-start | bytes 983044
  159.4 195.9 %all-gather.5.cloned.1.call-start = ((), (), s32[]{:S(2)}) async-start(), calls=%async_computation.5 | async-start | bytes 4259840 | tf_op jit(solution)/shard_map/all_gather | solution.py:80
  236.7 179.7 %all-reduce.7.cloned.1.call-start = ((), (), s32[]{:S(2)}) async-start(), calls=%async_computation.7 | async-start | bytes 524288
Sparse Core Ops, SparseCore 0:
  11.6 128.1 all-gather.2
  159.5 41.7 all-reduce.4
  236.9 118.3 all-gather.4
  374.8 41.5 all-reduce.6
where the time goes:
time: 428 us; the launch traced here: 427 us
  waiting for transfers between devices  305 us (71%)
  blocking collectives  51.5 us (12%)
  local copies, waits for them, and re-layouts  30.4 us (7%)
  between operations  14 us (3%)
  matrix products  13.9 us (3%)
  other arithmetic  12.1 us (3%)
    all_gather x1, waiting for transfers between devices, body(): lax.all_gather(right_side, 'row', axis=0, tiled=True)  128 us
    all_gather x1, waiting for transfers between devices, body(): lax.all_gather(right_moved, 'row', axis=1, tiled=True)  94.3 us
    unnamed x6, waiting for transfers between devices  82.4 us
    all_to_all x1, blocking collectives, body(): lax.all_to_all(spread_right, 'row', split_axis=1, concat_axis=0, tiled=True)  23.1 us
    all_to_all x1, blocking collectives, body(): lax.all_to_all(spread_left, 'row', split_axis=1, concat_axis=0, tiled=True)  14.8 us
    all_gather x1, local copies, waits for them, and re-layouts, body(): lax.all_gather(right_side, 'row', axis=0, tiled=True)  12.9 us
    all_gather x1, local copies, waits for them, and re-layouts, body(): lax.all_gather(right_moved, 'row', axis=1, tiled=True)  12.9 us
  transfers between devices with their start and end apart: 4, of which 4 were waited for; matrix products, arithmetic and copies ran while one was open for 1% of the time, Pallas kernels for 0%

commit v1 on v0

v1 whole, which is shorter than its diff:
```python
import functools

import jax
import jax.numpy as jnp
from jax import lax
from jax.experimental import pallas as pl
from jax.experimental.pallas import tpu as pltpu
from jax.sharding import PartitionSpec as P

EPS = 1e-05
MESH = pl.DeviceIdType.MESH
NEAR = (8, 9, 7, 10, 6, 5, 11, 12, 4, 3, 13, 14, 2, 1, 15)
F32 = jnp.float32
BF16 = jnp.bfloat16
NT = (((1,), (1,)), ((), ()))
NN = (((1,), (0,)), ((), ()))


def dot(a, b, dims):
    return lax.dot_general(a, b, dims, preferred_element_type=F32)


def iota(shape, axis):
    return lax.broadcasted_iota(jnp.int32, shape, axis)


def onehot(cond):
    return jnp.where(cond, 1.0, 0.0).astype(BF16)


def column_of(p):
    return (
        32 * ((p // 4) % 2)
        + 16 * ((p // 2) % 2)
        + 4 * (p // 16)
        + 2 * (p % 2)
        + (p // 8) % 2
    )


def eye(n):
    return onehot(iota((n, n), 0) == iota((n, n), 1))


def norm_t(v):
    mean = jnp.mean(v, axis=0, keepdims=True)
    centered = v - mean
    var = jnp.mean(centered * centered, axis=0, keepdims=True)
    return centered * lax.rsqrt(var + EPS)


def transposed_weight(w, lo):
    return dot(eye(128), w[:, lo : lo + 128], NT).astype(BF16)


def tiles_of(t):
    lo = t[:, :128].reshape(16, 8, 128)
    hi = t[:, 128:].reshape(16, 8, 128)
    return jnp.concatenate([lo, hi], axis=1).astype(BF16)


def kernel(
    pair, mask, wp, wo, out,
    xb, mb, wpb, wob, wt, p_t, gate,
    send1, recv1, scratch, la0, ra0, lb0, rb0, la1, ra1, lb1, rb1, osend, orecv,
    lsem, s1s, s1r, l2s, l2r, r2s, r2r, os, orr,
):
    row = lax.axis_index("row")
    q = lax.axis_index("ka")
    g = row // 4
    x = row % 4
    s = x * 4 + q

    barrier = pltpu.get_barrier_semaphore()
    for d in NEAR:
        pl.semaphore_signal(
            barrier, inc=1, device_id=(((g + d) % 16) * 4 + x, q), device_id_type=MESH
        )
        t = (s + d) % 16
        pl.semaphore_signal(
            barrier, inc=1, device_id=(g * 4 + t // 4, t % 4), device_id_type=MESH
        )
    loads = [
        pltpu.make_async_copy(a, b, lsem.at[i])
        for i, (a, b) in enumerate(((pair, xb), (mask, mb), (wp, wpb), (wo, wob)))
    ]
    for c in loads:
        c.start()
    for c in loads:
        c.wait()

    for u in range(2):
        for blk in range(5):
            wt[u, blk] = transposed_weight(wpb[u], blk * 128)
        wt[u, 5] = transposed_weight(wob[u], 0)

    n0 = iota((256, 256), 0)
    n1 = iota((256, 256), 1)
    perm_t = onehot(n1 == (n0 // 64) * 64 + column_of(n0 % 64))
    perm = onehot(n0 == (n1 // 64) * 64 + column_of(n1 % 64))
    moved = dot(perm_t, xb[...].reshape(256, 128), NN).astype(BF16)
    p_t[...] = dot(eye(128), moved, NT)
    tokens = jnp.broadcast_to(mb[...].astype(F32), (16, 256)).astype(BF16)
    m_row = dot(tokens, onehot(n0 == 4 * row + n1 // 64), NN)[0:1]
    m_col = dot(tokens, onehot(n0 == 64 * q + column_of(n1 % 64)), NN)[0:1]
    m_pair = m_row * m_col

    def project(u):
        normed = norm_t(p_t[...]).astype(BF16)
        ga = dot(wt[u, 0], normed, NN)
        va = dot(wt[u, 1], normed, NN)
        send1[u, :, 0] = tiles_of(jax.nn.sigmoid(ga) * va * m_pair)
        gb = dot(wt[u, 2], normed, NN)
        vb = dot(wt[u, 3], normed, NN)
        send1[u, :, 1] = tiles_of(jax.nn.sigmoid(gb) * vb * m_pair)

    def gate_of(u):
        normed = norm_t(p_t[...]).astype(BF16)
        gate[...] = jax.nn.sigmoid(dot(wt[u, 4], normed, NN))

    def exchange1(src, dst, ssem, rsem):
        for d in NEAR:
            t = (g + d) % 16
            pltpu.make_async_remote_copy(
                src.at[t], dst.at[g], ssem, rsem, device_id=(t * 4 + x, q), device_id_type=MESH
            ).start()
        dst[g] = src[g]

    def wait_bytes(buf, count, ssem, rsem, send):
        part = buf.at[pl.ds(0, count)]
        c = pltpu.make_async_remote_copy(
            part, part, ssem, rsem, device_id=(g * 4 + (x + 1) % 4, q), device_id_type=MESH
        )
        if send:
            c.wait_send()
        else:
            c.wait_recv()

    low = iota((32, 128), 1) < 64

    def pairs(u, side, cp):
        f = scratch.at[side]
        xa = f[pl.ds(2 * cp, 32, stride=8), :]
        xb_ = f[pl.ds(2 * cp + 1, 32, stride=8), :]
        even = jnp.where(low, xa, pltpu.roll(xb_, 64, 1))
        odd = jnp.where(low, pltpu.roll(xa, 64, 1), xb_)
        return even, odd

    def spread(u, side):
        v = recv1[u, :, side]
        scratch[side] = v.astype(F32).reshape(256, 128)

    def send_all16(src, by_x, dst, ssem, rsem):
        for d in NEAR:
            t = (s + d) % 16
            tx = t // 4
            tq = t % 4
            pltpu.make_async_remote_copy(
                src.at[tx] if by_x else src.at[tq], dst.at[s], ssem, rsem,
                device_id=(g * 4 + tx, tq), device_id_type=MESH,
            ).start()
        dst[s] = src[x] if by_x else src[q]

    def finish(u):
        hb = orecv[u].astype(F32)
        summed = jnp.concatenate(
            [hb[:, :8].reshape(128, 128), hb[:, 8:].reshape(128, 128)], axis=1
        )
        xn = norm_t(summed).astype(BF16)
        upd = dot(wt[u, 5], xn, NN)
        return (p_t[...] + gate[...] * upd).astype(BF16)

    def emit_sums(cp, oa0, oa1):
        c0 = jnp.where(low, oa0, pltpu.roll(oa1, 64, 1))
        c1 = jnp.where(low, pltpu.roll(oa0, 64, 1), oa1)
        scratch[2, pl.ds(2 * cp, 32, stride=8), :] = c0
        scratch[2, pl.ds(2 * cp + 1, 32, stride=8), :] = c1

    def send_sums(u):
        osend[u] = scratch[2].reshape(16, 16, 128).astype(BF16)
        exchange1(osend.at[u], orecv.at[u], os.at[u], orr.at[u])

    project(0)
    pl.semaphore_wait(barrier, 30)
    exchange1(send1.at[0], recv1.at[0], s1s.at[0], s1r.at[0])
    gate_of(0)
    wait_bytes(recv1.at[0], 15, s1s.at[0], s1r.at[0], False)

    spread(0, 0)
    for cp in range(4):
        even, odd = pairs(0, 0, cp)
        la0[cp] = jnp.concatenate([even, odd], axis=0).astype(BF16)
    for d in (2, 3, 1):
        t = (q + d) % 4
        pltpu.make_async_remote_copy(
            la0, lb0.at[q], l2s.at[0], l2r.at[0], device_id=(row, t), device_id_type=MESH
        ).start()
    lb0[q] = la0[...]
    spread(0, 1)
    for cp in range(4):
        even, odd = pairs(0, 1, cp)
        for j in range(4):
            ra0[j, cp] = jnp.concatenate(
                [even[8 * j : 8 * j + 8], odd[8 * j : 8 * j + 8]], axis=0
            ).astype(BF16)
    send_all16(ra0, False, rb0, r2s.at[0], r2r.at[0])
    wait_bytes(lb0, 3, l2s.at[0], l2r.at[0], False)
    wait_bytes(rb0, 15, r2s.at[0], r2r.at[0], False)

    low64 = iota((64, 128), 1) < 64
    zero = jnp.zeros((64, 128), BF16)
    for cp in range(4):
        a = jnp.concatenate([lb0[k, cp] for k in range(4)], axis=1)
        cols = []
        for k in range(4):
            b = jnp.concatenate([rb0[4 * j + k, cp] for j in range(4)], axis=0)
            cols.append(
                jnp.concatenate([jnp.where(low64, b, zero), jnp.where(low64, zero, b)], axis=0)
            )
        o = dot(a, jnp.concatenate(cols, axis=1), NT)
        emit_sums(cp, o[:32], o[32:])
    send_sums(0)
    wait_bytes(orecv.at[0], 15, os.at[0], orr.at[0], False)
    p_t[...] = finish(0).astype(F32)

    project(1)
    exchange1(send1.at[1], recv1.at[1], s1s.at[1], s1r.at[1])
    gate_of(1)
    wait_bytes(recv1.at[1], 15, s1s.at[1], s1r.at[1], False)

    spread(1, 0)
    pick = onehot(iota((64, 128), 0) == iota((64, 128), 1) % 64)
    for cp in range(4):
        even, odd = pairs(1, 0, cp)
        m = jnp.concatenate([even, odd], axis=0).astype(BF16)
        m2 = jnp.concatenate([jnp.where(low64, m, zero), jnp.where(low64, zero, m)], axis=0)
        t = dot(pick, m2, NT).astype(BF16)
        for k in range(4):
            la1[k, cp] = t[16 * k : 16 * k + 16]
    send_all16(la1, True, lb1, l2s.at[1], l2r.at[1])
    spread(1, 1)
    for cp in range(4):
        even, odd = pairs(1, 1, cp)
        ra1[cp] = jnp.concatenate([even, odd], axis=0).astype(BF16)
    for d in (2, 3, 1):
        t = (x + d) % 4
        pltpu.make_async_remote_copy(
            ra1, rb1.at[x], r2s.at[1], r2r.at[1], device_id=(g * 4 + t, q), device_id_type=MESH
        ).start()
    rb1[x] = ra1[...]
    wait_bytes(lb1, 15, l2s.at[1], l2r.at[1], False)
    wait_bytes(rb1, 3, r2s.at[1], r2r.at[1], False)

    for cp in range(4):
        a = jnp.concatenate(
            [jnp.concatenate([lb1[4 * j + k, cp] for k in range(4)], axis=0) for j in range(4)],
            axis=1,
        )
        rows = []
        for j in range(4):
            b = rb1[j, cp]
            rows += [jnp.where(low64, b, zero), jnp.where(low64, zero, b)]
        o = dot(a, jnp.concatenate(rows, axis=0), NN).reshape(4, 2, 8, 128)
        emit_sums(cp, o[:, 0].reshape(32, 128), o[:, 1].reshape(32, 128))
    send_sums(1)
    wait_bytes(orecv.at[1], 15, os.at[1], orr.at[1], False)
    final = finish(1)
    out[...] = dot(perm, final, NT).astype(BF16).reshape(4, 64, 128)

    for u in range(2):
        wait_bytes(recv1.at[u], 15, s1s.at[u], s1r.at[u], True)
        wait_bytes(orecv.at[u], 15, os.at[u], orr.at[u], True)
    wait_bytes(lb0, 3, l2s.at[0], l2r.at[0], True)
    wait_bytes(rb0, 15, r2s.at[0], r2r.at[0], True)
    wait_bytes(lb1, 15, l2s.at[1], l2r.at[1], True)
    wait_bytes(rb1, 3, r2s.at[1], r2r.at[1], True)


def body(pair, token_mask, w_proj, w_out):
    any_spec = pl.BlockSpec(memory_space=pl.ANY)
    vm = pltpu.VMEM
    dma = pltpu.SemaphoreType.DMA
    return pl.pallas_call(
        kernel,
        out_shape=jax.ShapeDtypeStruct((4, 64, 128), BF16),
        in_specs=[any_spec] * 4,
        out_specs=pl.BlockSpec(memory_space=pltpu.VMEM),
        scratch_shapes=[
            vm((4, 64, 128), BF16),
            vm((1, 256), jnp.int32),
            vm((2, 128, 640), BF16),
            vm((2, 128, 128), BF16),
            vm((2, 6, 128, 128), BF16),
            vm((128, 256), F32),
            vm((128, 256), F32),
            vm((2, 16, 2, 16, 128), BF16),
            vm((2, 16, 2, 16, 128), BF16),
            vm((3, 256, 128), F32),
            vm((4, 64, 128), BF16),
            vm((4, 4, 16, 128), BF16),
            vm((4, 4, 64, 128), BF16),
            vm((16, 4, 16, 128), BF16),
            vm((4, 4, 16, 128), BF16),
            vm((4, 64, 128), BF16),
            vm((16, 4, 16, 128), BF16),
            vm((4, 4, 64, 128), BF16),
            vm((2, 16, 16, 128), BF16),
            vm((2, 16, 16, 128), BF16),
            dma((4,)),
        ]
        + [dma((2,))] * 8,
        compiler_params=pltpu.CompilerParams(
            collective_id=0, has_side_effects=True, vmem_limit_bytes=40 * 2**20
        ),
        name="triangles",
    )(pair, token_mask.reshape(1, 256), w_proj, w_out)


def solution(mesh):
    return jax.shard_map(
        body,
        mesh=mesh,
        in_specs=(P("row", "ka", None), P(), P(), P()),
        out_specs=P("row", "ka", None),
        check_vma=False,
    )
```

time: 428 us -> 53.1 us (0.12)
  waiting for transfers between devices: 305 us -> 0 us
  blocking collectives: 51.5 us -> 0 us
  Pallas kernels: 0 us -> 48.2 us
  local copies, waits for them, and re-layouts: 30.4 us -> 3.96 us
  between operations: 14 us -> 0.01 us
  matrix products: 13.9 us -> 0 us
  other arithmetic: 12.1 us -> 0 us
    all_gather x2 -> x0, waiting for transfers between devices: 222 us -> none  [the longest x1 128 us: body(): lax.all_gather(right_side, 'row', axis=0, tiled=True)]
    unnamed x6 -> x0, waiting for transfers between devices: 82.4 us -> none
    all_to_all x4 -> x0, blocking collectives: 51.5 us -> none  [the longest x1 23.1 us: body(): lax.all_to_all(spread_right, 'row', split_axis=1, concat_axis=0, tiled=True)]
    pallas_call x0 -> x1, Pallas kernels: none -> 48.2 us  [body(): pl.pallas_call(kernel, out_shape=jax.ShapeDtypeStruct((4, 64, 128), BF16)...]
    all_gather x2 -> x0, local copies, waits for them, and re-layouts: 25.8 us -> none  [the longest x1 12.9 us: body(): lax.all_gather(right_side, 'row', axis=0, tiled=True)]
    dot_general x6 -> x0, matrix products: 13.9 us -> none  [the longest x1 5.68 us: body(): jnp.einsum('ikc,jkc->ijc', left_side, lax.all_gather(right_side, 'row', a...]
    reduce_sum x7 -> x0, other arithmetic: 6.24 us -> none  [the longest x4 3.33 us: normalize(): variance = jnp.mean(centered * centered, axis=-1, keepdims=True)]
  transfers between devices with their start and end apart: 4 -> 0, of which waited for: 4 -> 0; matrix products, arithmetic and copies ran while one was open for 1% -> 0% of each run, Pallas kernels for 0% -> 0%
where the time goes in v1:
time: 53.1 us; the launch traced here: 52.2 us
  Pallas kernels  48.2 us (91%)
  local copies, waits for them, and re-layouts  3.96 us (7%)
    pallas_call x1, Pallas kernels, body(): pl.pallas_call(kernel, out_shape=jax.ShapeDtypeStruct((4, 64, 128), BF16)...  48.2 us
    unnamed x9, local copies, waits for them, and re-layouts  3.96 us

profile of v1, /device:TPU:1, one launch (start us, length us, event | category | flops | bytes accessed | tf_op | source)
XLA Modules:
  0.0 52.2 jit_solution(9214011330816613809)
XLA Ops:
  0.0 0.0 copy-start.3
  0.0 0.7 %copy-done.3 = s32[256]{0:T(256)S(1)} copy-done((s32[256]{0:T(256)S(1)}, s32[256]{0:T(256)}, u32[]{:S(2)}) %copy-start.3) | copy-done | bytes 1048
  0.7 0.0 copy-start
  0.7 1.0 %copy-done = bf16[2,128,640]{2,1,0:T(8,128)(2,1)S(1)} copy-done((bf16[2,128,640]{2,1,0:T(8,128)(2,1)S(1)}, bf16[2,128,640]{2,1,0:T(8,128)(2,1)}, u32[]{:S(2)}) %copy-start) | copy-done | bytes 327704
  1.7 0.0 copy-start.1
  1.7 0.8 %copy-done.1 = bf16[4,64,128]{2,1,0:T(8,128)(2,1)S(1)} copy-done((bf16[4,64,128]{2,1,0:T(8,128)(2,1)S(1)}, bf16[4,64,128]{2,1,0:T(8,128)(2,1)}, u32[]{:S(2)}) %copy-start.1) | copy-done | bytes 65560
  2.5 0.0 copy-start.2
  2.5 0.8 %copy-done.2 = bf16[2,128,128]{2,1,0:T(8,128)(2,1)S(1)} copy-done((bf16[2,128,128]{2,1,0:T(8,128)(2,1)S(1)}, bf16[2,128,128]{2,1,0:T(8,128)(2,1)}, u32[]{:S(2)}) %copy-start.2) | copy-done | bytes 65560
  3.3 48.2 %triangles.1 = bf16[4,64,128]{2,1,0:T(8,128)(2,1)S(1)} custom-call(bf16[4,64,128]{2,1,0:T(8,128)(2,1)S(1)} %copy-done.1, s32[1,256]{1,0:T(1,128)S(1)} %bitcast.1, bf16[2,128,640]{2,1,0:T(8,128)(2,1)S(1)} %copy-done, bf16[2,128,128]{2,1,0:T(8,128)(2,1)S(1)} %copy-done.2), custom_call_target="tpu_custom_call" | custom-call | tf_op jit(solution)/shard_map/triangles/pallas_call | solution.py:283
  51.6 0.6 %copy.6 = bf16[4,64,128]{2,1,0:T(8,128)(2,1)} copy(bf16[4,64,128]{2,1,0:T(8,128)(2,1)S(1)} %triangles.1) | data formatting | bytes 131072
Async XLA Ops:
  0.0 0.7 %copy-start.3 = (s32[256]{0:T(256)S(1)}, s32[256]{0:T(256)}, u32[]{:S(2)}) copy-start(s32[256]{0:T(256)} %param.5) | copy-start | bytes 3076
  0.7 1.0 %copy-start = (bf16[2,128,640]{2,1,0:T(8,128)(2,1)S(1)}, bf16[2,128,640]{2,1,0:T(8,128)(2,1)}, u32[]{:S(2)}) copy-start(bf16[2,128,640]{2,1,0:T(8,128)(2,1)} %wp.1) | copy-start | bytes 983044
  1.7 0.8 %copy-start.1 = (bf16[4,64,128]{2,1,0:T(8,128)(2,1)S(1)}, bf16[4,64,128]{2,1,0:T(8,128)(2,1)}, u32[]{:S(2)}) copy-start(bf16[4,64,128]{2,1,0:T(8,128)(2,1)} %pair.1) | copy-start | bytes 196612
  2.5 0.8 %copy-start.2 = (bf16[2,128,128]{2,1,0:T(8,128)(2,1)S(1)}, bf16[2,128,128]{2,1,0:T(8,128)(2,1)}, u32[]{:S(2)}) copy-start(bf16[2,128,128]{2,1,0:T(8,128)(2,1)} %wo.1) | copy-start | bytes 196612

commit v2 on v1

--- a/solution.py
+++ b/solution.py
@@ -63,13 +63,16 @@
     pair, mask, wp, wo, out,
     xb, mb, wpb, wob, wt, p_t, gate,
     send1, recv1, scratch, la0, ra0, lb0, rb0, la1, ra1, lb1, rb1, osend, orecv,
-    lsem, s1s, s1r, l2s, l2r, r2s, r2r, os, orr,
+    lsem, s1s, s1r, l2s, l2r, cs, cr, r2s, r2r, os, orr,
 ):
     row = lax.axis_index("row")
     q = lax.axis_index("ka")
     g = row // 4
     x = row % 4
     s = x * 4 + q
+    core = q % 2
+    mate = q + 1 - 2 * core
+    over = (q + 2) % 4
 
     barrier = pltpu.get_barrier_semaphore()
     for d in NEAR:
@@ -105,14 +108,18 @@
     m_col = dot(tokens, onehot(n0 == 64 * q + column_of(n1 % 64)), NN)[0:1]
     m_pair = m_row * m_col
 
-    def project(u):
+    def project(u, send):
         normed = norm_t(p_t[...]).astype(BF16)
         ga = dot(wt[u, 0], normed, NN)
         va = dot(wt[u, 1], normed, NN)
-        send1[u, :, 0] = tiles_of(jax.nn.sigmoid(ga) * va * m_pair)
+        send1[2 * u] = tiles_of(jax.nn.sigmoid(ga) * va * m_pair)
+        if send:
+            stage1(2 * u)
         gb = dot(wt[u, 2], normed, NN)
         vb = dot(wt[u, 3], normed, NN)
-        send1[u, :, 1] = tiles_of(jax.nn.sigmoid(gb) * vb * m_pair)
+        send1[2 * u + 1] = tiles_of(jax.nn.sigmoid(gb) * vb * m_pair)
+        if send:
+            stage1(2 * u + 1)
 
     def gate_of(u):
         normed = norm_t(p_t[...]).astype(BF16)
@@ -126,6 +133,12 @@
             ).start()
         dst[g] = src[g]
 
+    def stage1(i):
+        exchange1(send1.at[i], recv1.at[i], s1s.at[i], s1r.at[i])
+
+    def stage1_wait(i, send):
+        wait_bytes(recv1.at[i], 15, s1s.at[i], s1r.at[i], send)
+
     def wait_bytes(buf, count, ssem, rsem, send):
         part = buf.at[pl.ds(0, count)]
         c = pltpu.make_async_remote_copy(
@@ -147,19 +160,34 @@
         return even, odd
 
     def spread(u, side):
-        v = recv1[u, :, side]
-        scratch[side] = v.astype(F32).reshape(256, 128)
-
-    def send_all16(src, by_x, dst, ssem, rsem):
+        stage1_wait(2 * u + side, False)
+        scratch[side] = recv1[2 * u + side].astype(F32).reshape(256, 128)
+
+    def send_mate(src, dst, ssem, rsem):
+        return pltpu.make_async_remote_copy(
+            src, dst, ssem, rsem, device_id=(row, mate), device_id_type=MESH
+        )
+
+    def send_all16(src, dst, ssem, rsem):
         for d in NEAR:
             t = (s + d) % 16
             tx = t // 4
             tq = t % 4
             pltpu.make_async_remote_copy(
-                src.at[tx] if by_x else src.at[tq], dst.at[s], ssem, rsem,
-                device_id=(g * 4 + tx, tq), device_id_type=MESH,
+                src.at[tq], dst.at[s], ssem, rsem, device_id=(g * 4 + tx, tq), device_id_type=MESH
             ).start()
-        dst[s] = src[x] if by_x else src[q]
+        dst[s] = src[q]
+
+    def send_all8(src, dst, ssem, rsem):
+        half = x * 2 + q // 2
+        for d in (4, 5, 3, 2, 6, 1, 7):
+            t = (half + d) % 8
+            tx = t // 2
+            tq = (t % 2) * 2 + core
+            pltpu.make_async_remote_copy(
+                src.at[tx], dst.at[half], ssem, rsem, device_id=(g * 4 + tx, tq), device_id_type=MESH
+            ).start()
+        dst[half] = src[x]
 
     def finish(u):
         hb = orecv[u].astype(F32)
@@ -180,21 +208,22 @@
         osend[u] = scratch[2].reshape(16, 16, 128).astype(BF16)
         exchange1(osend.at[u], orecv.at[u], os.at[u], orr.at[u])
 
-    project(0)
+    project(0, False)
     pl.semaphore_wait(barrier, 30)
-    exchange1(send1.at[0], recv1.at[0], s1s.at[0], s1r.at[0])
+    stage1(0)
+    stage1(1)
     gate_of(0)
-    wait_bytes(recv1.at[0], 15, s1s.at[0], s1r.at[0], False)
 
     spread(0, 0)
     for cp in range(4):
         even, odd = pairs(0, 0, cp)
         la0[cp] = jnp.concatenate([even, odd], axis=0).astype(BF16)
-    for d in (2, 3, 1):
-        t = (q + d) % 4
-        pltpu.make_async_remote_copy(
-            la0, lb0.at[q], l2s.at[0], l2r.at[0], device_id=(row, t), device_id_type=MESH
-        ).start()
+    across = pltpu.make_async_remote_copy(
+        la0, lb0.at[q], l2s.at[0], l2r.at[0], device_id=(row, over), device_id_type=MESH
+    )
+    across.start()
+    to_mate = send_mate(la0, lb0.at[q], cs.at[0], cr.at[0])
+    to_mate.start()
     lb0[q] = la0[...]
     spread(0, 1)
     for cp in range(4):
@@ -203,9 +232,13 @@
             ra0[j, cp] = jnp.concatenate(
                 [even[8 * j : 8 * j + 8], odd[8 * j : 8 * j + 8]], axis=0
             ).astype(BF16)
-    send_all16(ra0, False, rb0, r2s.at[0], r2r.at[0])
-    wait_bytes(lb0, 3, l2s.at[0], l2r.at[0], False)
+    send_all16(ra0, rb0, r2s.at[0], r2r.at[0])
+    across.wait_recv()
+    passed = send_mate(lb0.at[over], lb0.at[over], cs.at[1], cr.at[1])
+    passed.start()
+    to_mate.wait_recv()
     wait_bytes(rb0, 15, r2s.at[0], r2r.at[0], False)
+    passed.wait_recv()
 
     low64 = iota((64, 128), 1) < 64
     zero = jnp.zeros((64, 128), BF16)
@@ -223,10 +256,8 @@
     wait_bytes(orecv.at[0], 15, os.at[0], orr.at[0], False)
     p_t[...] = finish(0).astype(F32)
 
-    project(1)
-    exchange1(send1.at[1], recv1.at[1], s1s.at[1], s1r.at[1])
+    project(1, True)
     gate_of(1)
-    wait_bytes(recv1.at[1], 15, s1s.at[1], s1r.at[1], False)
 
     spread(1, 0)
     pick = onehot(iota((64, 128), 0) == iota((64, 128), 1) % 64)
@@ -237,7 +268,7 @@
         t = dot(pick, m2, NT).astype(BF16)
         for k in range(4):
             la1[k, cp] = t[16 * k : 16 * k + 16]
-    send_all16(la1, True, lb1, l2s.at[1], l2r.at[1])
+    send_all8(la1, lb1.at[core], l2s.at[1], l2r.at[1])
     spread(1, 1)
     for cp in range(4):
         even, odd = pairs(1, 1, cp)
@@ -248,12 +279,15 @@
             ra1, rb1.at[x], r2s.at[1], r2r.at[1], device_id=(g * 4 + t, q), device_id_type=MESH
         ).start()
     rb1[x] = ra1[...]
-    wait_bytes(lb1, 15, l2s.at[1], l2r.at[1], False)
+    wait_bytes(lb1.at[core], 7, l2s.at[1], l2r.at[1], False)
+    passed1 = send_mate(lb1.at[core], lb1.at[core], cs.at[2], cr.at[2])
+    passed1.start()
     wait_bytes(rb1, 3, r2s.at[1], r2r.at[1], False)
+    passed1.wait_recv()
 
     for cp in range(4):
         a = jnp.concatenate(
-            [jnp.concatenate([lb1[4 * j + k, cp] for k in range(4)], axis=0) for j in range(4)],
+            [jnp.concatenate([lb1[k % 2, 2 * j + k // 2, cp] for k in range(4)], axis=0) for j in range(4)],
             axis=1,
         )
         rows = []
@@ -267,13 +301,19 @@
     final = finish(1)
     out[...] = dot(perm, final, NT).astype(BF16).reshape(4, 64, 128)
 
-    for u in range(2):
-        wait_bytes(recv1.at[u], 15, s1s.at[u], s1r.at[u], True)
-        wait_bytes(orecv.at[u], 15, os.at[u], orr.at[u], True)
-    wait_bytes(lb0, 3, l2s.at[0], l2r.at[0], True)
+    stage1_wait(0, True)
+    stage1_wait(1, True)
+    across.wait_send()
+    to_mate.wait_send()
+    passed.wait_send()
     wait_bytes(rb0, 15, r2s.at[0], r2r.at[0], True)
-    wait_bytes(lb1, 15, l2s.at[1], l2r.at[1], True)
+    wait_bytes(orecv.at[0], 15, os.at[0], orr.at[0], True)
+    stage1_wait(2, True)
+    stage1_wait(3, True)
+    wait_bytes(lb1.at[core], 7, l2s.at[1], l2r.at[1], True)
+    passed1.wait_send()
     wait_bytes(rb1, 3, r2s.at[1], r2r.at[1], True)
+    wait_bytes(orecv.at[1], 15, os.at[1], orr.at[1], True)
 
 
 def body(pair, token_mask, w_proj, w_out):
@@ -282,7 +322,7 @@
     dma = pltpu.SemaphoreType.DMA
     return pl.pallas_call(
         kernel,
-        out_shape=jax.ShapeDtypeStruct((4, 64, 128), BF16),
+        out_shape=pltpu.VMEM((4, 64, 128), BF16),
         in_specs=[any_spec] * 4,
         out_specs=pl.BlockSpec(memory_space=pltpu.VMEM),
         scratch_shapes=[
@@ -293,8 +333,8 @@
             vm((2, 6, 128, 128), BF16),
             vm((128, 256), F32),
             vm((128, 256), F32),
-            vm((2, 16, 2, 16, 128), BF16),
-            vm((2, 16, 2, 16, 128), BF16),
+            vm((4, 16, 16, 128), BF16),
+            vm((4, 16, 16, 128), BF16),
             vm((3, 256, 128), F32),
             vm((4, 64, 128), BF16),
             vm((4, 4, 16, 128), BF16),
@@ -302,15 +342,21 @@
             vm((16, 4, 16, 128), BF16),
             vm((4, 4, 16, 128), BF16),
             vm((4, 64, 128), BF16),
-            vm((16, 4, 16, 128), BF16),
+            vm((2, 8, 4, 16, 128), BF16),
             vm((4, 4, 64, 128), BF16),
             vm((2, 16, 16, 128), BF16),
             vm((2, 16, 16, 128), BF16),
             dma((4,)),
+            dma((4,)),
+            dma((4,)),
+            dma((2,)),
+            dma((2,)),
+            dma((3,)),
+            dma((3,)),
         ]
-        + [dma((2,))] * 8,
+        + [dma((2,))] * 4,
         compiler_params=pltpu.CompilerParams(
-            collective_id=0, has_side_effects=True, vmem_limit_bytes=40 * 2**20
+            collective_id=0, has_side_effects=True, vmem_limit_bytes=60 * 2**20
         ),
         name="triangles",
     )(pair, token_mask.reshape(1, 256), w_proj, w_out)

time: 53.1 us -> 49.5 us (0.932); the launches traced: 52.2 us -> 49.4 us
  local copies, waits for them, and re-layouts: 3.96 us -> 0.63 us
  Pallas kernels: 48.2 us -> 48.8 us
    unnamed x9 -> x1, local copies, waits for them, and re-layouts: 3.96 us -> 0.63 us
    pallas_call x1, Pallas kernels: 48.2 us -> 48.8 us  [body(): pl.pallas_call(kernel, out_shape=pltpu.VMEM((4, 64, 128), BF16), in_specs...]
where the time goes in v2:
time: 49.5 us; the launch traced here: 49.4 us
  Pallas kernels  48.8 us (99%)
  local copies, waits for them, and re-layouts  0.63 us (1%)
    pallas_call x1, Pallas kernels, body(): pl.pallas_call(kernel, out_shape=pltpu.VMEM((4, 64, 128), BF16), in_specs...  48.8 us

profile of v2, /device:TPU:1, one launch (start us, length us, event | category | flops | bytes accessed | tf_op | source)
XLA Modules:
  0.0 49.4 jit_solution(14943550288954908261)
XLA Ops:
  0.0 48.8 %triangles.1 = bf16[4,64,128]{2,1,0:T(8,128)(2,1)S(1)} custom-call(bf16[4,64,128]{2,1,0:T(8,128)(2,1)} %pair.1, s32[1,256]{1,0:T(1,128)} %bitcast.1, bf16[2,128,640]{2,1,0:T(8,128)(2,1)} %wp.1, bf16[2,128,128]{2,1,0:T(8,128)(2,1)} %wo.1), custom_call_target="tpu_custom_call" | custom-call | tf_op jit(solution)/shard_map/triangles/pallas_call | solution.py:323
  48.8 0.6 %copy.6 = bf16[4,64,128]{2,1,0:T(8,128)(2,1)} copy(bf16[4,64,128]{2,1,0:T(8,128)(2,1)S(1)} %triangles.1) | data formatting | bytes 131072

commit v3 on v2

--- a/solution.py
+++ b/solution.py
@@ -9,7 +9,8 @@
 
 EPS = 1e-05
 MESH = pl.DeviceIdType.MESH
-NEAR = (8, 9, 7, 10, 6, 5, 11, 12, 4, 3, 13, 14, 2, 1, 15)
+FAR1 = tuple((dz, e) for dz in (4, 3, 5, 2, 6, 1, 7, 0) for e in (1, 0))[:-1]
+FAR2 = (10, 8, 14, 11, 9, 15, 2, 6, 12, 13, 3, 7, 4, 5, 1)
 F32 = jnp.float32
 BF16 = jnp.bfloat16
 NT = (((1,), (1,)), ((), ()))
@@ -29,13 +30,7 @@
 
 
 def column_of(p):
-    return (
-        32 * ((p // 4) % 2)
-        + 16 * ((p // 2) % 2)
-        + 4 * (p // 16)
-        + 2 * (p % 2)
-        + (p // 8) % 2
-    )
+    return 32 * ((p // 4) % 2) + 8 * (p // 16) + 4 * ((p // 2) % 2) + 2 * (p % 2) + (p // 8) % 2
 
 
 def eye(n):
@@ -67,22 +62,29 @@
 ):
     row = lax.axis_index("row")
     q = lax.axis_index("ka")
-    g = row // 4
-    x = row % 4
+    z = row // 8
+    lo = row % 2
+    g = z * 2 + lo
+    x = (row // 2) % 4
     s = x * 4 + q
     core = q % 2
     mate = q + 1 - 2 * core
     over = (q + 2) % 4
 
+    def row_of(group, v):
+        return (group // 2) * 8 + v * 2 + group % 2
+
+    group1 = [((z + dz) % 8) * 2 + (lo + e) % 2 for dz, e in FAR1]
+    group2 = []
+    for m in FAR2:
+        v = ((x // 2 + m // 8) % 2) * 2 + (x + m // 4) % 2
+        group2.append((v, ((q // 2 + m // 2) % 2) * 2 + (q + m) % 2))
+
     barrier = pltpu.get_barrier_semaphore()
-    for d in NEAR:
-        pl.semaphore_signal(
-            barrier, inc=1, device_id=(((g + d) % 16) * 4 + x, q), device_id_type=MESH
-        )
-        t = (s + d) % 16
-        pl.semaphore_signal(
-            barrier, inc=1, device_id=(g * 4 + t // 4, t % 4), device_id_type=MESH
-        )
+    for t in group1:
+        pl.semaphore_signal(barrier, inc=1, device_id=(row_of(t, x), q), device_id_type=MESH)
+    for v, t in group2:
+        pl.semaphore_signal(barrier, inc=1, device_id=(row_of(g, v), t), device_id_type=MESH)
     loads = [
         pltpu.make_async_copy(a, b, lsem.at[i])
         for i, (a, b) in enumerate(((pair, xb), (mask, mb), (wp, wpb), (wo, wob)))
@@ -108,28 +110,23 @@
     m_col = dot(tokens, onehot(n0 == 64 * q + column_of(n1 % 64)), NN)[0:1]
     m_pair = m_row * m_col
 
-    def project(u, send):
+    def project(u):
         normed = norm_t(p_t[...]).astype(BF16)
         ga = dot(wt[u, 0], normed, NN)
         va = dot(wt[u, 1], normed, NN)
-        send1[2 * u] = tiles_of(jax.nn.sigmoid(ga) * va * m_pair)
-        if send:
-            stage1(2 * u)
+        send1[u, :, 0] = tiles_of(jax.nn.sigmoid(ga) * va * m_pair)
         gb = dot(wt[u, 2], normed, NN)
         vb = dot(wt[u, 3], normed, NN)
-        send1[2 * u + 1] = tiles_of(jax.nn.sigmoid(gb) * vb * m_pair)
-        if send:
-            stage1(2 * u + 1)
+        send1[u, :, 1] = tiles_of(jax.nn.sigmoid(gb) * vb * m_pair)
 
     def gate_of(u):
         normed = norm_t(p_t[...]).astype(BF16)
         gate[...] = jax.nn.sigmoid(dot(wt[u, 4], normed, NN))
 
     def exchange1(src, dst, ssem, rsem):
-        for d in NEAR:
-            t = (g + d) % 16
+        for t in group1:
             pltpu.make_async_remote_copy(
-                src.at[t], dst.at[g], ssem, rsem, device_id=(t * 4 + x, q), device_id_type=MESH
+                src.at[t], dst.at[g], ssem, rsem, device_id=(row_of(t, x), q), device_id_type=MESH
             ).start()
         dst[g] = src[g]
 
@@ -142,7 +139,7 @@
     def wait_bytes(buf, count, ssem, rsem, send):
         part = buf.at[pl.ds(0, count)]
         c = pltpu.make_async_remote_copy(
-            part, part, ssem, rsem, device_id=(g * 4 + (x + 1) % 4, q), device_id_type=MESH
+            part, part, ssem, rsem, device_id=(row, mate), device_id_type=MESH
         )
         if send:
             c.wait_send()
@@ -160,8 +157,7 @@
         return even, odd
 
     def spread(u, side):
-        stage1_wait(2 * u + side, False)
-        scratch[side] = recv1[2 * u + side].astype(F32).reshape(256, 128)
+        scratch[side] = recv1[u, :, side].astype(F32).reshape(256, 128)
 
     def send_mate(src, dst, ssem, rsem):
         return pltpu.make_async_remote_copy(
@@ -169,24 +165,20 @@
         )
 
     def send_all16(src, dst, ssem, rsem):
-        for d in NEAR:
-            t = (s + d) % 16
-            tx = t // 4
-            tq = t % 4
+        for tx, tq in group2:
             pltpu.make_async_remote_copy(
-                src.at[tq], dst.at[s], ssem, rsem, device_id=(g * 4 + tx, tq), device_id_type=MESH
+                src.at[tq], dst.at[s], ssem, rsem, device_id=(row_of(g, tx), tq), device_id_type=MESH
             ).start()
         dst[s] = src[q]
 
     def send_all8(src, dst, ssem, rsem):
         half = x * 2 + q // 2
-        for d in (4, 5, 3, 2, 6, 1, 7):
-            t = (half + d) % 8
-            tx = t // 2
-            tq = (t % 2) * 2 + core
-            pltpu.make_async_remote_copy(
-                src.at[tx], dst.at[half], ssem, rsem, device_id=(g * 4 + tx, tq), device_id_type=MESH
-            ).start()
+        for m, (tx, tq) in zip(FAR2, group2):
+            if m % 2 == 0:
+                pltpu.make_async_remote_copy(
+                    src.at[tx], dst.at[half], ssem, rsem,
+                    device_id=(row_of(g, tx), tq), device_id_type=MESH,
+                ).start()
         dst[half] = src[x]
 
     def finish(u):
@@ -208,11 +200,11 @@
         osend[u] = scratch[2].reshape(16, 16, 128).astype(BF16)
         exchange1(osend.at[u], orecv.at[u], os.at[u], orr.at[u])
 
-    project(0, False)
+    project(0)
     pl.semaphore_wait(barrier, 30)
     stage1(0)
-    stage1(1)
     gate_of(0)
+    stage1_wait(0, False)
 
     spread(0, 0)
     for cp in range(4):
@@ -256,9 +248,10 @@
     wait_bytes(orecv.at[0], 15, os.at[0], orr.at[0], False)
     p_t[...] = finish(0).astype(F32)
 
-    project(1, True)
+    project(1)
+    stage1(1)
     gate_of(1)
-
+    stage1_wait(1, False)
     spread(1, 0)
     pick = onehot(iota((64, 128), 0) == iota((64, 128), 1) % 64)
     for cp in range(4):
@@ -273,11 +266,12 @@
     for cp in range(4):
         even, odd = pairs(1, 1, cp)
         ra1[cp] = jnp.concatenate([even, odd], axis=0).astype(BF16)
-    for d in (2, 3, 1):
-        t = (x + d) % 4
-        pltpu.make_async_remote_copy(
-            ra1, rb1.at[x], r2s.at[1], r2r.at[1], device_id=(g * 4 + t, q), device_id_type=MESH
-        ).start()
+    for m, (t, _) in zip(FAR2, group2):
+        if m % 4 == 0:
+            pltpu.make_async_remote_copy(
+                ra1, rb1.at[x], r2s.at[1], r2r.at[1],
+                device_id=(row_of(g, t), q), device_id_type=MESH,
+            ).start()
     rb1[x] = ra1[...]
     wait_bytes(lb1.at[core], 7, l2s.at[1], l2r.at[1], False)
     passed1 = send_mate(lb1.at[core], lb1.at[core], cs.at[2], cr.at[2])
@@ -302,14 +296,12 @@
     out[...] = dot(perm, final, NT).astype(BF16).reshape(4, 64, 128)
 
     stage1_wait(0, True)
-    stage1_wait(1, True)
     across.wait_send()
     to_mate.wait_send()
     passed.wait_send()
     wait_bytes(rb0, 15, r2s.at[0], r2r.at[0], True)
     wait_bytes(orecv.at[0], 15, os.at[0], orr.at[0], True)
-    stage1_wait(2, True)
-    stage1_wait(3, True)
+    stage1_wait(1, True)
     wait_bytes(lb1.at[core], 7, l2s.at[1], l2r.at[1], True)
     passed1.wait_send()
     wait_bytes(rb1, 3, r2s.at[1], r2r.at[1], True)
@@ -333,8 +325,8 @@
             vm((2, 6, 128, 128), BF16),
             vm((128, 256), F32),
             vm((128, 256), F32),
-            vm((4, 16, 16, 128), BF16),
-            vm((4, 16, 16, 128), BF16),
+            vm((2, 16, 2, 16, 128), BF16),
+            vm((2, 16, 2, 16, 128), BF16),
             vm((3, 256, 128), F32),
             vm((4, 64, 128), BF16),
             vm((4, 4, 16, 128), BF16),
@@ -347,8 +339,8 @@
             vm((2, 16, 16, 128), BF16),
             vm((2, 16, 16, 128), BF16),
             dma((4,)),
-            dma((4,)),
-            dma((4,)),
+            dma((2,)),
+            dma((2,)),
             dma((2,)),
             dma((2,)),
             dma((3,)),

time: 49.5 us -> 46.3 us (0.935)
  Pallas kernels: 48.8 us -> 45.5 us
    pallas_call x1, Pallas kernels: 48.8 us -> 45.5 us  [body(): pl.pallas_call(kernel, out_shape=pltpu.VMEM((4, 64, 128), BF16), in_specs...]
where the time goes in v3:
time: 46.3 us; the launch traced here: 46.2 us
  Pallas kernels  45.5 us (98%)
  local copies, waits for them, and re-layouts  0.63 us (1%)
    pallas_call x1, Pallas kernels, body(): pl.pallas_call(kernel, out_shape=pltpu.VMEM((4, 64, 128), BF16), in_specs...  45.5 us

profile of v3, /device:TPU:1, one launch (start us, length us, event | category | flops | bytes accessed | tf_op | source)
XLA Modules:
  0.0 46.2 jit_solution(6348245512849818967)
XLA Ops:
  0.0 45.5 %triangles.1 = bf16[4,64,128]{2,1,0:T(8,128)(2,1)S(1)} custom-call(bf16[4,64,128]{2,1,0:T(8,128)(2,1)} %pair.1, s32[1,256]{1,0:T(1,128)} %bitcast.1, bf16[2,128,640]{2,1,0:T(8,128)(2,1)} %wp.1, bf16[2,128,128]{2,1,0:T(8,128)(2,1)} %wo.1), custom_call_target="tpu_custom_call" | custom-call | tf_op jit(solution)/shard_map/triangles/pallas_call | solution.py:315
  45.5 0.6 %copy.6 = bf16[4,64,128]{2,1,0:T(8,128)(2,1)} copy(bf16[4,64,128]{2,1,0:T(8,128)(2,1)S(1)} %triangles.1) | data formatting | bytes 131072

commit v4 on v3

--- a/solution.py
+++ b/solution.py
@@ -8,9 +8,10 @@
 from jax.sharding import PartitionSpec as P
 
 EPS = 1e-05
+PE, PH, PL = 1, 4, 2
 MESH = pl.DeviceIdType.MESH
 FAR1 = tuple((dz, e) for dz in (4, 3, 5, 2, 6, 1, 7, 0) for e in (1, 0))[:-1]
-FAR2 = (10, 8, 14, 11, 9, 15, 2, 6, 12, 13, 3, 7, 4, 5, 1)
+FAR2 = (12, 13, 14, 15, 6, 7, 8, 9, 4, 5, 10, 11, 2, 3, 1)
 F32 = jnp.float32
 BF16 = jnp.bfloat16
 NT = (((1,), (1,)), ((), ()))
@@ -30,7 +31,8 @@
 
 
 def column_of(p):
-    return 32 * ((p // 4) % 2) + 8 * (p // 16) + 4 * ((p // 2) % 2) + 2 * (p % 2) + (p // 8) % 2
+    v = PH * (p // 32) + PL * ((p // 16) % 2) + PE * ((p // 2) % 2)
+    return 32 * ((p // 4) % 2) + 4 * v + 2 * (p % 2) + (p // 8) % 2
 
 
 def eye(n):
@@ -58,21 +60,22 @@
     pair, mask, wp, wo, out,
     xb, mb, wpb, wob, wt, p_t, gate,
     send1, recv1, scratch, la0, ra0, lb0, rb0, la1, ra1, lb1, rb1, osend, orecv,
-    lsem, s1s, s1r, l2s, l2r, cs, cr, r2s, r2r, os, orr,
+    lsem, s1s, s1r, l2s, l2r, l1s, l1r, cs, cr, r2s, r2r, os, orr,
 ):
     row = lax.axis_index("row")
     q = lax.axis_index("ka")
     z = row // 8
-    lo = row % 2
+    lo = (row // PE) % 2
     g = z * 2 + lo
-    x = (row // 2) % 4
+    x = ((row // PH) % 2) * 2 + (row // PL) % 2
     s = x * 4 + q
     core = q % 2
     mate = q + 1 - 2 * core
     over = (q + 2) % 4
+    side = q // 2
 
     def row_of(group, v):
-        return (group // 2) * 8 + v * 2 + group % 2
+        return (group // 2) * 8 + (v // 2) * PH + (v % 2) * PL + (group % 2) * PE
 
     group1 = [((z + dz) % 8) * 2 + (lo + e) % 2 for dz, e in FAR1]
     group2 = []
@@ -171,15 +174,47 @@
             ).start()
         dst[s] = src[q]
 
-    def send_all8(src, dst, ssem, rsem):
-        half = x * 2 + q // 2
-        for m, (tx, tq) in zip(FAR2, group2):
-            if m % 2 == 0:
-                pltpu.make_async_remote_copy(
-                    src.at[tx], dst.at[half], ssem, rsem,
-                    device_id=(row_of(g, tx), tq), device_id_type=MESH,
-                ).start()
-        dst[half] = src[x]
+    def send_left1():
+        for v in range(4):
+            for y in range(2):
+                copy = pltpu.make_async_remote_copy(
+                    la1.at[v], lb1.at[core, side, x], l1s, l1r.at[side],
+                    device_id=(row_of(g, v), y * 2 + core), device_id_type=MESH,
+                )
+                pl.when((x != v) | (side != y))(copy.start)
+        pltpu.make_async_copy(la1.at[x], lb1.at[core, side, x], l1r.at[side]).start()
+
+    def send_right1():
+        for v in range(4):
+            copy = pltpu.make_async_remote_copy(
+                ra1, rb1.at[x], r2s.at[1], r2r.at[1],
+                device_id=(row_of(g, v), q), device_id_type=MESH,
+            )
+            pl.when(x != v)(copy.start)
+
+    def send_sums_half(c):
+        part = sums_rows(c)
+        osend[1, 8 * c : 8 * c + 8] = part.reshape(8, 16, 128).astype(BF16)
+
+        def out(t):
+            return pltpu.make_async_remote_copy(
+                osend.at[1, t], orecv.at[1, g], os.at[1], orr.at[1],
+                device_id=(row_of(t, x), q), device_id_type=MESH,
+            )
+
+        for i in (4, 5, 3, 2, 6, 7, 1):
+            out(8 * c + (g + i) % 8).start()
+
+        @pl.when(g // 8 != c)
+        def _():
+            out(8 * c + g % 8).start()
+
+        @pl.when(g // 8 == c)
+        def _():
+            orecv[1, g] = osend[1, g]
+
+    def sums_rows(c):
+        return scratch[2, 128 * c : 128 * c + 128]
 
     def finish(u):
         hb = orecv[u].astype(F32)
@@ -190,11 +225,13 @@
         upd = dot(wt[u, 5], xn, NN)
         return (p_t[...] + gate[...] * upd).astype(BF16)
 
-    def emit_sums(cp, oa0, oa1):
+    def emit_sums(cp, oa0, oa1, base=0):
+        n = oa0.shape[0]
+        low = iota((n, 128), 1) < 64
         c0 = jnp.where(low, oa0, pltpu.roll(oa1, 64, 1))
         c1 = jnp.where(low, pltpu.roll(oa0, 64, 1), oa1)
-        scratch[2, pl.ds(2 * cp, 32, stride=8), :] = c0
-        scratch[2, pl.ds(2 * cp + 1, 32, stride=8), :] = c1
+        scratch[2, pl.ds(base + 2 * cp, n, stride=8), :] = c0
+        scratch[2, pl.ds(base + 2 * cp + 1, n, stride=8), :] = c1
 
     def send_sums(u):
         osend[u] = scratch[2].reshape(16, 16, 128).astype(BF16)
@@ -261,36 +298,44 @@
         t = dot(pick, m2, NT).astype(BF16)
         for k in range(4):
             la1[k, cp] = t[16 * k : 16 * k + 16]
-    send_all8(la1, lb1.at[core], l2s.at[1], l2r.at[1])
+    @pl.when(side == 0)
+    def _():
+        send_left1()
+
     spread(1, 1)
     for cp in range(4):
         even, odd = pairs(1, 1, cp)
         ra1[cp] = jnp.concatenate([even, odd], axis=0).astype(BF16)
-    for m, (t, _) in zip(FAR2, group2):
-        if m % 4 == 0:
-            pltpu.make_async_remote_copy(
-                ra1, rb1.at[x], r2s.at[1], r2r.at[1],
-                device_id=(row_of(g, t), q), device_id_type=MESH,
-            ).start()
+    send_right1()
+
+    @pl.when(side == 1)
+    def _():
+        send_left1()
+
     rb1[x] = ra1[...]
-    wait_bytes(lb1.at[core], 7, l2s.at[1], l2r.at[1], False)
-    passed1 = send_mate(lb1.at[core], lb1.at[core], cs.at[2], cr.at[2])
-    passed1.start()
-    wait_bytes(rb1, 3, r2s.at[1], r2r.at[1], False)
-    passed1.wait_recv()
-
-    for cp in range(4):
-        a = jnp.concatenate(
-            [jnp.concatenate([lb1[k % 2, 2 * j + k // 2, cp] for k in range(4)], axis=0) for j in range(4)],
-            axis=1,
-        )
-        rows = []
-        for j in range(4):
-            b = rb1[j, cp]
-            rows += [jnp.where(low64, b, zero), jnp.where(low64, zero, b)]
-        o = dot(a, jnp.concatenate(rows, axis=0), NN).reshape(4, 2, 8, 128)
-        emit_sums(cp, o[:, 0].reshape(32, 128), o[:, 1].reshape(32, 128))
-    send_sums(1)
+    passed1 = []
+    for c in range(2):
+        got = lb1.at[core, c]
+        pltpu.make_async_remote_copy(
+            got, got, l1s, l1r.at[c], device_id=(row, mate), device_id_type=MESH
+        ).wait_recv()
+        passed1.append(send_mate(got, got, cs.at[2 + c], cr.at[2 + c]))
+        passed1[c].start()
+        if c == 0:
+            wait_bytes(rb1, 3, r2s.at[1], r2r.at[1], False)
+        passed1[c].wait_recv()
+        for cp in range(4):
+            a = jnp.concatenate(
+                [jnp.concatenate([lb1[k, c, j, cp] for k in range(2)], axis=0) for j in range(4)],
+                axis=1,
+            )
+            rows = []
+            for j in range(4):
+                b = rb1[j, cp]
+                rows += [jnp.where(low64, b, zero), jnp.where(low64, zero, b)]
+            o = dot(a, jnp.concatenate(rows, axis=0), NN).reshape(2, 2, 8, 128)
+            emit_sums(cp, o[:, 0].reshape(16, 128), o[:, 1].reshape(16, 128), 128 * c)
+        send_sums_half(c)
     wait_bytes(orecv.at[1], 15, os.at[1], orr.at[1], False)
     final = finish(1)
     out[...] = dot(perm, final, NT).astype(BF16).reshape(4, 64, 128)
@@ -302,8 +347,9 @@
     wait_bytes(rb0, 15, r2s.at[0], r2r.at[0], True)
     wait_bytes(orecv.at[0], 15, os.at[0], orr.at[0], True)
     stage1_wait(1, True)
-    wait_bytes(lb1.at[core], 7, l2s.at[1], l2r.at[1], True)
-    passed1.wait_send()
+    wait_bytes(rb0, 7, l1s, l1r.at[0], True)
+    for c in passed1:
+        c.wait_send()
     wait_bytes(rb1, 3, r2s.at[1], r2r.at[1], True)
     wait_bytes(orecv.at[1], 15, os.at[1], orr.at[1], True)
 
@@ -334,17 +380,19 @@
             vm((16, 4, 16, 128), BF16),
             vm((4, 4, 16, 128), BF16),
             vm((4, 64, 128), BF16),
-            vm((2, 8, 4, 16, 128), BF16),
+            vm((2, 2, 4, 4, 16, 128), BF16),
             vm((4, 4, 64, 128), BF16),
             vm((2, 16, 16, 128), BF16),
             vm((2, 16, 16, 128), BF16),
             dma((4,)),
             dma((2,)),
             dma((2,)),
+            dma((1,)),
+            dma((1,)),
+            dma,
             dma((2,)),
-            dma((2,)),
-            dma((3,)),
-            dma((3,)),
+            dma((4,)),
+            dma((4,)),
         ]
         + [dma((2,))] * 4,
         compiler_params=pltpu.CompilerParams(

time: 46.3 us -> 46 us (level); the launches traced: 46.2 us -> 45.3 us
  Pallas kernels: 45.5 us -> 44.6 us
    pallas_call x1, Pallas kernels: 45.5 us -> 44.6 us  [body(): pl.pallas_call(kernel, out_shape=pltpu.VMEM((4, 64, 128), BF16), in_specs...]
where the time goes in v4:
time: 46 us; the launch traced here: 45.3 us
  Pallas kernels  44.6 us (97%)
  local copies, waits for them, and re-layouts  0.63 us (1%)
    pallas_call x1, Pallas kernels, body(): pl.pallas_call(kernel, out_shape=pltpu.VMEM((4, 64, 128), BF16), in_specs...  44.6 us

profile of v4, /device:TPU:1, one launch (start us, length us, event | category | flops | bytes accessed | tf_op | source)
XLA Modules:
  0.0 45.3 jit_solution(4588583121175021287)
XLA Ops:
  0.0 44.6 %triangles.1 = bf16[4,64,128]{2,1,0:T(8,128)(2,1)S(1)} custom-call(bf16[4,64,128]{2,1,0:T(8,128)(2,1)} %pair.1, s32[1,256]{1,0:T(1,128)} %bitcast.1, bf16[2,128,640]{2,1,0:T(8,128)(2,1)} %wp.1, bf16[2,128,128]{2,1,0:T(8,128)(2,1)} %wo.1), custom_call_target="tpu_custom_call" | custom-call | tf_op jit(solution)/shard_map/triangles/pallas_call | solution.py:361
  44.6 0.6 %copy.6 = bf16[4,64,128]{2,1,0:T(8,128)(2,1)} copy(bf16[4,64,128]{2,1,0:T(8,128)(2,1)S(1)} %triangles.1) | data formatting | bytes 131072

commit v5 on v4

--- a/solution.py
+++ b/solution.py
@@ -58,9 +58,9 @@
 
 def kernel(
     pair, mask, wp, wo, out,
-    xb, mb, wpb, wob, wt, p_t, gate,
-    send1, recv1, scratch, la0, ra0, lb0, rb0, la1, ra1, lb1, rb1, osend, orecv,
-    lsem, s1s, s1r, l2s, l2r, l1s, l1r, cs, cr, r2s, r2r, os, orr,
+    xb, mb, wpb, wob, wt, p_t, gate, perm,
+    send1, recv1, scratch, la0, ra0, lb0, rb0, la1, rdir, lb1, rb1, osend, orecv,
+    lsem, s1s, s1r, rds, rdr, l2s, l2r, l1s, l1r, cs, cr, r2s, r2r, os, orr,
 ):
     row = lax.axis_index("row")
     q = lax.axis_index("ka")
@@ -77,6 +77,7 @@
     def row_of(group, v):
         return (group // 2) * 8 + (v // 2) * PH + (v % 2) * PL + (group % 2) * PE
 
+    classes = [((x // 2 + f // 2) % 2) * 2 + (x + f) % 2 for f in range(4)]
     group1 = [((z + dz) % 8) * 2 + (lo + e) % 2 for dz, e in FAR1]
     group2 = []
     for m in FAR2:
@@ -97,15 +98,12 @@
     for c in loads:
         c.wait()
 
-    for u in range(2):
-        for blk in range(5):
-            wt[u, blk] = transposed_weight(wpb[u], blk * 128)
-        wt[u, 5] = transposed_weight(wob[u], 0)
+    for blk in range(4):
+        wt[0, blk] = transposed_weight(wpb[0], blk * 128)
 
     n0 = iota((256, 256), 0)
     n1 = iota((256, 256), 1)
     perm_t = onehot(n1 == (n0 // 64) * 64 + column_of(n0 % 64))
-    perm = onehot(n0 == (n1 // 64) * 64 + column_of(n1 % 64))
     moved = dot(perm_t, xb[...].reshape(256, 128), NN).astype(BF16)
     p_t[...] = dot(eye(128), moved, NT)
     tokens = jnp.broadcast_to(mb[...].astype(F32), (16, 256)).astype(BF16)
@@ -135,6 +133,41 @@
 
     def stage1(i):
         exchange1(send1.at[i], recv1.at[i], s1s.at[i], s1r.at[i])
+
+    def stage1_left():
+        for t in group1:
+            pltpu.make_async_remote_copy(
+                send1.at[1, t, 0], recv1.at[1, g, 0], s1s.at[1], s1r.at[1],
+                device_id=(row_of(t, x), q), device_id_type=MESH,
+            ).start()
+        recv1[1, g, 0] = send1[1, g, 0]
+
+    def direct_right():
+        for d in (3, 2, 1, 0):
+            v = classes[d]
+
+            def step(i, carry):
+                t = (g + 8 + ((i + 1) // 2) * (1 - 2 * (i % 2))) % 16
+                pltpu.make_async_remote_copy(
+                    send1.at[1, t, 1], rdir.at[x, g], rds, rdr.at[x],
+                    device_id=(row_of(t, v), q), device_id_type=MESH,
+                ).start()
+                return carry
+
+            lax.fori_loop(0, 15 if d == 0 else 16, step, 0)
+        rdir[x, g] = send1[1, g, 1]
+
+    def right_from(d):
+        v = classes[d]
+        n = 15 if d == 0 else 16
+        part = osend.at[0, pl.ds(0, n)]
+        pltpu.make_async_remote_copy(
+            part, part, rds, rdr.at[v], device_id=(row, mate), device_id_type=MESH
+        ).wait_recv()
+        scratch[1] = rdir[v].astype(F32).reshape(256, 128)
+        for cp in range(4):
+            even, odd = pairs(1, 1, cp)
+            rb1[v, cp] = jnp.concatenate([even, odd], axis=0).astype(BF16)
 
     def stage1_wait(i, send):
         wait_bytes(recv1.at[i], 15, s1s.at[i], s1r.at[i], send)
@@ -184,14 +217,6 @@
                 pl.when((x != v) | (side != y))(copy.start)
         pltpu.make_async_copy(la1.at[x], lb1.at[core, side, x], l1r.at[side]).start()
 
-    def send_right1():
-        for v in range(4):
-            copy = pltpu.make_async_remote_copy(
-                ra1, rb1.at[x], r2s.at[1], r2r.at[1],
-                device_id=(row_of(g, v), q), device_id_type=MESH,
-            )
-            pl.when(x != v)(copy.start)
-
     def send_sums_half(c):
         part = sums_rows(c)
         osend[1, 8 * c : 8 * c + 8] = part.reshape(8, 16, 128).astype(BF16)
@@ -240,7 +265,9 @@
     project(0)
     pl.semaphore_wait(barrier, 30)
     stage1(0)
+    wt[0, 4] = transposed_weight(wpb[0], 512)
     gate_of(0)
+    wt[0, 5] = transposed_weight(wob[0], 0)
     stage1_wait(0, False)
 
     spread(0, 0)
@@ -282,13 +309,17 @@
         o = dot(a, jnp.concatenate(cols, axis=1), NT)
         emit_sums(cp, o[:32], o[32:])
     send_sums(0)
+    for blk in range(5):
+        wt[1, blk] = transposed_weight(wpb[1], blk * 128)
+    wt[1, 5] = transposed_weight(wob[1], 0)
     wait_bytes(orecv.at[0], 15, os.at[0], orr.at[0], False)
     p_t[...] = finish(0).astype(F32)
 
     project(1)
-    stage1(1)
+    stage1_left()
+    direct_right()
     gate_of(1)
-    stage1_wait(1, False)
+    wait_bytes(osend.at[0], 15, s1s.at[1], s1r.at[1], False)
     spread(1, 0)
     pick = onehot(iota((64, 128), 0) == iota((64, 128), 1) % 64)
     for cp in range(4):
@@ -298,21 +329,9 @@
         t = dot(pick, m2, NT).astype(BF16)
         for k in range(4):
             la1[k, cp] = t[16 * k : 16 * k + 16]
-    @pl.when(side == 0)
-    def _():
-        send_left1()
-
-    spread(1, 1)
-    for cp in range(4):
-        even, odd = pairs(1, 1, cp)
-        ra1[cp] = jnp.concatenate([even, odd], axis=0).astype(BF16)
-    send_right1()
-
-    @pl.when(side == 1)
-    def _():
-        send_left1()
-
-    rb1[x] = ra1[...]
+    send_left1()
+    for d in range(3):
+        right_from(d)
     passed1 = []
     for c in range(2):
         got = lb1.at[core, c]
@@ -322,7 +341,7 @@
         passed1.append(send_mate(got, got, cs.at[2 + c], cr.at[2 + c]))
         passed1[c].start()
         if c == 0:
-            wait_bytes(rb1, 3, r2s.at[1], r2r.at[1], False)
+            right_from(3)
         passed1[c].wait_recv()
         for cp in range(4):
             a = jnp.concatenate(
@@ -336,9 +355,10 @@
             o = dot(a, jnp.concatenate(rows, axis=0), NN).reshape(2, 2, 8, 128)
             emit_sums(cp, o[:, 0].reshape(16, 128), o[:, 1].reshape(16, 128), 128 * c)
         send_sums_half(c)
+    perm[...] = onehot(n0 == (n1 // 64) * 64 + column_of(n1 % 64))
     wait_bytes(orecv.at[1], 15, os.at[1], orr.at[1], False)
     final = finish(1)
-    out[...] = dot(perm, final, NT).astype(BF16).reshape(4, 64, 128)
+    out[...] = dot(perm[...], final, NT).astype(BF16).reshape(4, 64, 128)
 
     stage1_wait(0, True)
     across.wait_send()
@@ -346,11 +366,12 @@
     passed.wait_send()
     wait_bytes(rb0, 15, r2s.at[0], r2r.at[0], True)
     wait_bytes(orecv.at[0], 15, os.at[0], orr.at[0], True)
-    stage1_wait(1, True)
+    wait_bytes(osend.at[0], 15, s1s.at[1], s1r.at[1], True)
     wait_bytes(rb0, 7, l1s, l1r.at[0], True)
     for c in passed1:
         c.wait_send()
-    wait_bytes(rb1, 3, r2s.at[1], r2r.at[1], True)
+    for n in (16, 16, 16, 15):
+        wait_bytes(osend.at[0], n, rds, rdr.at[0], True)
     wait_bytes(orecv.at[1], 15, os.at[1], orr.at[1], True)
 
 
@@ -371,6 +392,7 @@
             vm((2, 6, 128, 128), BF16),
             vm((128, 256), F32),
             vm((128, 256), F32),
+            vm((256, 256), BF16),
             vm((2, 16, 2, 16, 128), BF16),
             vm((2, 16, 2, 16, 128), BF16),
             vm((3, 256, 128), F32),
@@ -379,7 +401,7 @@
             vm((4, 4, 64, 128), BF16),
             vm((16, 4, 16, 128), BF16),
             vm((4, 4, 16, 128), BF16),
-            vm((4, 64, 128), BF16),
+            vm((4, 16, 16, 128), BF16),
             vm((2, 2, 4, 4, 16, 128), BF16),
             vm((4, 4, 64, 128), BF16),
             vm((2, 16, 16, 128), BF16),
@@ -387,6 +409,8 @@
             dma((4,)),
             dma((2,)),
             dma((2,)),
+            dma,
+            dma((4,)),
             dma((1,)),
             dma((1,)),
             dma,

time: 46 us -> 45.1 us (0.980); the launches traced: 45.3 us -> 45 us
  no operation moved by 1% of the time
where the time goes in v5:
time: 45.1 us; the launch traced here: 45 us
  Pallas kernels  44.4 us (98%)
  local copies, waits for them, and re-layouts  0.63 us (1%)
    pallas_call x1, Pallas kernels, body(): pl.pallas_call(kernel, out_shape=pltpu.VMEM((4, 64, 128), BF16), in_specs...  44.4 us

profile of v5, /device:TPU:1, one launch (start us, length us, event | category | flops | bytes accessed | tf_op | source)
XLA Modules:
  0.0 45.0 jit_solution(14095796700000786112)
XLA Ops:
  0.0 44.4 %triangles.1 = bf16[4,64,128]{2,1,0:T(8,128)(2,1)S(1)} custom-call(bf16[4,64,128]{2,1,0:T(8,128)(2,1)} %pair.1, s32[1,256]{1,0:T(1,128)} %bitcast.1, bf16[2,128,640]{2,1,0:T(8,128)(2,1)} %wp.1, bf16[2,128,128]{2,1,0:T(8,128)(2,1)} %wo.1), custom_call_target="tpu_custom_call" | custom-call | tf_op jit(solution)/shard_map/triangles/pallas_call | solution.py:382
  44.4 0.6 %copy.6 = bf16[4,64,128]{2,1,0:T(8,128)(2,1)} copy(bf16[4,64,128]{2,1,0:T(8,128)(2,1)S(1)} %triangles.1) | data formatting | bytes 131072

commit v6 on v5

--- a/solution.py
+++ b/solution.py
@@ -209,12 +209,12 @@
 
     def send_left1():
         for v in range(4):
-            for y in range(2):
+            for there in range(4):
                 copy = pltpu.make_async_remote_copy(
                     la1.at[v], lb1.at[core, side, x], l1s, l1r.at[side],
-                    device_id=(row_of(g, v), y * 2 + core), device_id_type=MESH,
+                    device_id=(row_of(g, v), there), device_id_type=MESH,
                 )
-                pl.when((x != v) | (side != y))(copy.start)
+                pl.when((x != v) | (q != there))(copy.start)
         pltpu.make_async_copy(la1.at[x], lb1.at[core, side, x], l1r.at[side]).start()
 
     def send_sums_half(c):
@@ -332,17 +332,10 @@
     send_left1()
     for d in range(3):
         right_from(d)
-    passed1 = []
     for c in range(2):
-        got = lb1.at[core, c]
-        pltpu.make_async_remote_copy(
-            got, got, l1s, l1r.at[c], device_id=(row, mate), device_id_type=MESH
-        ).wait_recv()
-        passed1.append(send_mate(got, got, cs.at[2 + c], cr.at[2 + c]))
-        passed1[c].start()
+        wait_bytes(rb0, 8, l1s, l1r.at[c], False)
         if c == 0:
             right_from(3)
-        passed1[c].wait_recv()
         for cp in range(4):
             a = jnp.concatenate(
                 [jnp.concatenate([lb1[k, c, j, cp] for k in range(2)], axis=0) for j in range(4)],
@@ -367,9 +360,7 @@
     wait_bytes(rb0, 15, r2s.at[0], r2r.at[0], True)
     wait_bytes(orecv.at[0], 15, os.at[0], orr.at[0], True)
     wait_bytes(osend.at[0], 15, s1s.at[1], s1r.at[1], True)
-    wait_bytes(rb0, 7, l1s, l1r.at[0], True)
-    for c in passed1:
-        c.wait_send()
+    wait_bytes(rb0, 15, l1s, l1r.at[0], True)
     for n in (16, 16, 16, 15):
         wait_bytes(osend.at[0], n, rds, rdr.at[0], True)
     wait_bytes(orecv.at[1], 15, os.at[1], orr.at[1], True)

time: 45.1 us -> 44.8 us (level)
  no operation moved by 1% of the time
where the time goes in v6:
time: 44.8 us; the launch traced here: 44.7 us
  Pallas kernels  44 us (98%)
  local copies, waits for them, and re-layouts  0.63 us (1%)
    pallas_call x1, Pallas kernels, body(): pl.pallas_call(kernel, out_shape=pltpu.VMEM((4, 64, 128), BF16), in_specs...  44 us

profile of v6, /device:TPU:1, one launch (start us, length us, event | category | flops | bytes accessed | tf_op | source)
XLA Modules:
  0.0 44.7 jit_solution(9143671780894815354)
XLA Ops:
  0.0 44.0 %triangles.1 = bf16[4,64,128]{2,1,0:T(8,128)(2,1)S(1)} custom-call(bf16[4,64,128]{2,1,0:T(8,128)(2,1)} %pair.1, s32[1,256]{1,0:T(1,128)} %bitcast.1, bf16[2,128,640]{2,1,0:T(8,128)(2,1)} %wp.1, bf16[2,128,128]{2,1,0:T(8,128)(2,1)} %wo.1), custom_call_target="tpu_custom_call" | custom-call | tf_op jit(solution)/shard_map/triangles/pallas_call | solution.py:373
  44.0 0.6 %copy.6 = bf16[4,64,128]{2,1,0:T(8,128)(2,1)} copy(bf16[4,64,128]{2,1,0:T(8,128)(2,1)S(1)} %triangles.1) | data formatting | bytes 131072

commit v7 on v6

--- a/solution.py
+++ b/solution.py
@@ -59,8 +59,8 @@
 def kernel(
     pair, mask, wp, wo, out,
     xb, mb, wpb, wob, wt, p_t, gate, perm,
-    send1, recv1, scratch, la0, ra0, lb0, rb0, la1, rdir, lb1, rb1, osend, orecv,
-    lsem, s1s, s1r, rds, rdr, l2s, l2r, l1s, l1r, cs, cr, r2s, r2r, os, orr,
+    send1, recv1, scratch, ldir, ra0, lb0, rb0, la1, rdir, lb1, rb1, osend, orecv,
+    lsem, s1s, s1r, ready, lds, ldr, rds, rdr, l1s, l1r, r2s, r2r, os, orr,
 ):
     row = lax.axis_index("row")
     q = lax.axis_index("ka")
@@ -131,9 +131,6 @@
             ).start()
         dst[g] = src[g]
 
-    def stage1(i):
-        exchange1(send1.at[i], recv1.at[i], s1s.at[i], s1r.at[i])
-
     def stage1_left():
         for t in group1:
             pltpu.make_async_remote_copy(
@@ -141,6 +138,35 @@
                 device_id=(row_of(t, x), q), device_id_type=MESH,
             ).start()
         recv1[1, g, 0] = send1[1, g, 0]
+
+    def wait_tiles(n, ssem, rsem, send):
+        wait_bytes(osend.at[0], n, ssem, rsem, send)
+
+    def stage1_right():
+        for t in group1:
+            pltpu.make_async_remote_copy(
+                send1.at[0, t, 1], recv1.at[0, g, 1], s1s.at[0], s1r.at[0],
+                device_id=(row_of(t, x), q), device_id_type=MESH,
+            ).start()
+        recv1[0, g, 1] = send1[0, g, 1]
+
+    def direct_left(there, n):
+        def step(i, carry):
+            t = (g + 8 + ((i + 1) // 2) * (1 - 2 * (i % 2))) % 16
+            pltpu.make_async_remote_copy(
+                send1.at[0, t, 0], ldir.at[q, g], lds, ldr.at[q],
+                device_id=(row_of(t, x), there), device_id_type=MESH,
+            ).start()
+            return carry
+
+        lax.fori_loop(0, n, step, 0)
+
+    def left_from(b, n):
+        wait_tiles(n, lds, ldr.at[b], False)
+        scratch[0] = ldir[b].astype(F32).reshape(256, 128)
+        for cp in range(4):
+            even, odd = pairs(0, 0, cp)
+            lb0[b, cp] = jnp.concatenate([even, odd], axis=0).astype(BF16)
 
     def direct_right():
         for d in (3, 2, 1, 0):
@@ -169,9 +195,6 @@
             even, odd = pairs(1, 1, cp)
             rb1[v, cp] = jnp.concatenate([even, odd], axis=0).astype(BF16)
 
-    def stage1_wait(i, send):
-        wait_bytes(recv1.at[i], 15, s1s.at[i], s1r.at[i], send)
-
     def wait_bytes(buf, count, ssem, rsem, send):
         part = buf.at[pl.ds(0, count)]
         c = pltpu.make_async_remote_copy(
@@ -195,11 +218,6 @@
     def spread(u, side):
         scratch[side] = recv1[u, :, side].astype(F32).reshape(256, 128)
 
-    def send_mate(src, dst, ssem, rsem):
-        return pltpu.make_async_remote_copy(
-            src, dst, ssem, rsem, device_id=(row, mate), device_id_type=MESH
-        )
-
     def send_all16(src, dst, ssem, rsem):
         for tx, tq in group2:
             pltpu.make_async_remote_copy(
@@ -264,23 +282,20 @@
 
     project(0)
     pl.semaphore_wait(barrier, 30)
-    stage1(0)
+    beside = (mate, over, (mate + 2) % 4)
+    for b in beside:
+        pl.semaphore_signal(ready, inc=1, device_id=(row, b), device_id_type=MESH)
+    stage1_right()
+    direct_left(q, 15)
+    ldir[q, g] = send1[0, g, 0]
+    pl.semaphore_wait(ready, 3)
+    for b in (beside[2], beside[1], beside[0]):
+        direct_left(b, 16)
     wt[0, 4] = transposed_weight(wpb[0], 512)
     gate_of(0)
     wt[0, 5] = transposed_weight(wob[0], 0)
-    stage1_wait(0, False)
-
-    spread(0, 0)
-    for cp in range(4):
-        even, odd = pairs(0, 0, cp)
-        la0[cp] = jnp.concatenate([even, odd], axis=0).astype(BF16)
-    across = pltpu.make_async_remote_copy(
-        la0, lb0.at[q], l2s.at[0], l2r.at[0], device_id=(row, over), device_id_type=MESH
-    )
-    across.start()
-    to_mate = send_mate(la0, lb0.at[q], cs.at[0], cr.at[0])
-    to_mate.start()
-    lb0[q] = la0[...]
+    wait_tiles(15, s1s.at[0], s1r.at[0], False)
+
     spread(0, 1)
     for cp in range(4):
         even, odd = pairs(0, 1, cp)
@@ -289,12 +304,10 @@
                 [even[8 * j : 8 * j + 8], odd[8 * j : 8 * j + 8]], axis=0
             ).astype(BF16)
     send_all16(ra0, rb0, r2s.at[0], r2r.at[0])
-    across.wait_recv()
-    passed = send_mate(lb0.at[over], lb0.at[over], cs.at[1], cr.at[1])
-    passed.start()
-    to_mate.wait_recv()
+    left_from(q, 15)
+    for b in beside:
+        left_from(b, 16)
     wait_bytes(rb0, 15, r2s.at[0], r2r.at[0], False)
-    passed.wait_recv()
 
     low64 = iota((64, 128), 1) < 64
     zero = jnp.zeros((64, 128), BF16)
@@ -353,10 +366,9 @@
     final = finish(1)
     out[...] = dot(perm[...], final, NT).astype(BF16).reshape(4, 64, 128)
 
-    stage1_wait(0, True)
-    across.wait_send()
-    to_mate.wait_send()
-    passed.wait_send()
+    wait_tiles(15, s1s.at[0], s1r.at[0], True)
+    for n in (16, 16, 16, 15):
+        wait_tiles(n, lds, ldr.at[0], True)
     wait_bytes(rb0, 15, r2s.at[0], r2r.at[0], True)
     wait_bytes(orecv.at[0], 15, os.at[0], orr.at[0], True)
     wait_bytes(osend.at[0], 15, s1s.at[1], s1r.at[1], True)
@@ -387,7 +399,7 @@
             vm((2, 16, 2, 16, 128), BF16),
             vm((2, 16, 2, 16, 128), BF16),
             vm((3, 256, 128), F32),
-            vm((4, 64, 128), BF16),
+            vm((4, 16, 16, 128), BF16),
             vm((4, 4, 16, 128), BF16),
             vm((4, 4, 64, 128), BF16),
             vm((16, 4, 16, 128), BF16),
@@ -400,14 +412,13 @@
             dma((4,)),
             dma((2,)),
             dma((2,)),
+            pltpu.SemaphoreType.REGULAR,
             dma,
             dma((4,)),
-            dma((1,)),
-            dma((1,)),
+            dma,
+            dma((4,)),
             dma,
             dma((2,)),
-            dma((4,)),
-            dma((4,)),
         ]
         + [dma((2,))] * 4,
         compiler_params=pltpu.CompilerParams(

time: 44.8 us -> 44.4 us (level)
  no operation moved by 1% of the time
where the time goes in v7:
time: 44.4 us; the launch traced here: 44.3 us
  Pallas kernels  43.7 us (98%)
  local copies, waits for them, and re-layouts  0.63 us (1%)
    pallas_call x1, Pallas kernels, body(): pl.pallas_call(kernel, out_shape=pltpu.VMEM((4, 64, 128), BF16), in_specs...  43.7 us

profile of v7, /device:TPU:1, one launch (start us, length us, event | category | flops | bytes accessed | tf_op | source)
XLA Modules:
  0.0 44.3 jit_solution(6903172648155701244)
XLA Ops:
  0.0 43.7 %triangles.1 = bf16[4,64,128]{2,1,0:T(8,128)(2,1)S(1)} custom-call(bf16[4,64,128]{2,1,0:T(8,128)(2,1)} %pair.1, s32[1,256]{1,0:T(1,128)} %bitcast.1, bf16[2,128,640]{2,1,0:T(8,128)(2,1)} %wp.1, bf16[2,128,128]{2,1,0:T(8,128)(2,1)} %wo.1), custom_call_target="tpu_custom_call" | custom-call | tf_op jit(solution)/shard_map/triangles/pallas_call | solution.py:385
  43.7 0.6 %copy.6 = bf16[4,64,128]{2,1,0:T(8,128)(2,1)} copy(bf16[4,64,128]{2,1,0:T(8,128)(2,1)S(1)} %triangles.1) | data formatting | bytes 131072

commit v8 on v7

--- a/solution.py
+++ b/solution.py
@@ -111,14 +111,10 @@
     m_col = dot(tokens, onehot(n0 == 64 * q + column_of(n1 % 64)), NN)[0:1]
     m_pair = m_row * m_col
 
-    def project(u):
-        normed = norm_t(p_t[...]).astype(BF16)
-        ga = dot(wt[u, 0], normed, NN)
-        va = dot(wt[u, 1], normed, NN)
-        send1[u, :, 0] = tiles_of(jax.nn.sigmoid(ga) * va * m_pair)
-        gb = dot(wt[u, 2], normed, NN)
-        vb = dot(wt[u, 3], normed, NN)
-        send1[u, :, 1] = tiles_of(jax.nn.sigmoid(gb) * vb * m_pair)
+    def project(u, normed, part):
+        gate_in = dot(wt[u, 2 * part], normed, NN)
+        value = dot(wt[u, 2 * part + 1], normed, NN)
+        send1[u, :, part] = tiles_of(jax.nn.sigmoid(gate_in) * value * m_pair)
 
     def gate_of(u):
         normed = norm_t(p_t[...]).astype(BF16)
@@ -280,7 +276,9 @@
         osend[u] = scratch[2].reshape(16, 16, 128).astype(BF16)
         exchange1(osend.at[u], orecv.at[u], os.at[u], orr.at[u])
 
-    project(0)
+    normed0 = norm_t(p_t[...]).astype(BF16)
+    project(0, normed0, 0)
+    project(0, normed0, 1)
     pl.semaphore_wait(barrier, 30)
     beside = (mate, over, (mate + 2) % 4)
     for b in beside:
@@ -328,8 +326,10 @@
     wait_bytes(orecv.at[0], 15, os.at[0], orr.at[0], False)
     p_t[...] = finish(0).astype(F32)
 
-    project(1)
+    normed1 = norm_t(p_t[...]).astype(BF16)
+    project(1, normed1, 0)
     stage1_left()
+    project(1, normed1, 1)
     direct_right()
     gate_of(1)
     wait_bytes(osend.at[0], 15, s1s.at[1], s1r.at[1], False)

time: 44.4 us -> 44.2 us (level)
  no operation moved by 1% of the time
where the time goes in v8:
time: 44.2 us; the launch traced here: 44.1 us
  Pallas kernels  43.4 us (98%)
  local copies, waits for them, and re-layouts  0.63 us (1%)
    pallas_call x1, Pallas kernels, body(): pl.pallas_call(kernel, out_shape=pltpu.VMEM((4, 64, 128), BF16), in_specs...  43.4 us

profile of v8, /device:TPU:1, one launch (start us, length us, event | category | flops | bytes accessed | tf_op | source)
XLA Modules:
  0.0 44.1 jit_solution(675304696341475962)
XLA Ops:
  0.0 43.4 %triangles.1 = bf16[4,64,128]{2,1,0:T(8,128)(2,1)S(1)} custom-call(bf16[4,64,128]{2,1,0:T(8,128)(2,1)} %pair.1, s32[1,256]{1,0:T(1,128)} %bitcast.1, bf16[2,128,640]{2,1,0:T(8,128)(2,1)} %wp.1, bf16[2,128,128]{2,1,0:T(8,128)(2,1)} %wo.1), custom_call_target="tpu_custom_call" | custom-call | tf_op jit(solution)/shard_map/triangles/pallas_call | solution.py:385
  43.5 0.6 %copy.6 = bf16[4,64,128]{2,1,0:T(8,128)(2,1)} copy(bf16[4,64,128]{2,1,0:T(8,128)(2,1)S(1)} %triangles.1) | data formatting | bytes 131072

commit v9 on v8

--- a/solution.py
+++ b/solution.py
@@ -345,10 +345,9 @@
     send_left1()
     for d in range(3):
         right_from(d)
+    right_from(3)
     for c in range(2):
         wait_bytes(rb0, 8, l1s, l1r.at[c], False)
-        if c == 0:
-            right_from(3)
         for cp in range(4):
             a = jnp.concatenate(
                 [jnp.concatenate([lb1[k, c, j, cp] for k in range(2)], axis=0) for j in range(4)],

time: 44.2 us -> 44.1 us (level)
  no operation moved by 1% of the time
where the time goes in v9:
time: 44.1 us; the launch traced here: 44 us
  Pallas kernels  43.3 us (98%)
  local copies, waits for them, and re-layouts  0.63 us (1%)
    pallas_call x1, Pallas kernels, body(): pl.pallas_call(kernel, out_shape=pltpu.VMEM((4, 64, 128), BF16), in_specs...  43.3 us

profile of v9, /device:TPU:1, one launch (start us, length us, event | category | flops | bytes accessed | tf_op | source)
XLA Modules:
  0.0 44.0 jit_solution(6395460253010096056)
XLA Ops:
  0.0 43.3 %triangles.1 = bf16[4,64,128]{2,1,0:T(8,128)(2,1)S(1)} custom-call(bf16[4,64,128]{2,1,0:T(8,128)(2,1)} %pair.1, s32[1,256]{1,0:T(1,128)} %bitcast.1, bf16[2,128,640]{2,1,0:T(8,128)(2,1)} %wp.1, bf16[2,128,128]{2,1,0:T(8,128)(2,1)} %wo.1), custom_call_target="tpu_custom_call" | custom-call | tf_op jit(solution)/shard_map/triangles/pallas_call | solution.py:384
  43.3 0.6 %copy.6 = bf16[4,64,128]{2,1,0:T(8,128)(2,1)} copy(bf16[4,64,128]{2,1,0:T(8,128)(2,1)S(1)} %triangles.1) | data formatting | bytes 131072
